TPU v7x, 32 devices: a whole 2x2x4 slice. The times are simulated.
32 devices in a mesh: seq: 16 (over z, y, x), head: 2 (over core).
Axes of the slice: x: 2, y: 2, z: 4, core: 2. Of those that a mesh axis runs over, the one named last changes fastest.
Arguments:
- hidden_in: bfloat16 [2, 4096, 1024], P(None, 'seq', 'head'), may hold values from -6 to 6
- doc_start: int32 [2, 4096], P(None, 'seq'), may hold values from 0 to 1, as said below
- norm_gain: bfloat16 [1024], P('head'), may hold values from 0.5 to 1.5
- proj_gate: bfloat16 [1024, 2048], P(None, 'head'), may hold values from -0.1875 to 0.1875
- proj_value: bfloat16 [1024, 2048], P(None, 'head'), may hold values from -0.1875 to 0.1875
- proj_maps: bfloat16 [1024, 256], P(None, 'head'), may hold values from -0.1875 to 0.1875
- proj_step: bfloat16 [1024, 32], P(None, 'head'), may hold values from -0.1875 to 0.1875
- conv_value: float32 [4, 2048], P(None, 'head'), may hold values from -3 to 3
- value_bias: float32 [2048], P('head'), may hold values from -1.5 to 1.5
- conv_maps: float32 [4, 256], P(None, 'head'), may hold values from -3 to 3
- maps_bias: float32 [256], P('head'), may hold values from -1.5 to 1.5
- step_bias: float32 [32], P('head'), may hold values from -4 to -2
- decay_log: float32 [32], P('head'), may hold values from -12 to 1
- skip_gain: float32 [32], P('head'), may hold values from 0.5 to 1.5
- gate_gain: float32 [2048], P('head'), may hold values from 0.5 to 1.5
- proj_out: bfloat16 [2048, 1024], P('head'), may hold values from -0.125 to 0.125
- out_grad: bfloat16 [2, 4096, 1024], P(None, 'seq', 'head'), may hold values from -6 to 6
Outputs:
- mixed_out: bfloat16 [2, 4096, 1024], P(None, 'seq', 'head')
- input_grad: float32 [2, 4096, 1024], P(None, 'seq', 'head')
- grad_norm_gain: float32 [1024], P('head')
- grad_proj_gate: float32 [1024, 2048], P(None, 'head')
- grad_proj_value: float32 [1024, 2048], P(None, 'head')
- grad_proj_maps: float32 [1024, 256], P(None, 'head')
- grad_proj_step: float32 [1024, 32], P(None, 'head')
- grad_conv_value: float32 [4, 2048], P(None, 'head')
- grad_value_bias: float32 [2048], P('head')
- grad_conv_maps: float32 [4, 256], P(None, 'head')
- grad_maps_bias: float32 [256], P('head')
- grad_step_bias: float32 [32], P('head')
- grad_decay_log: float32 [32], P('head')
- grad_skip_gain: float32 [32], P('head')
- grad_gate_gain: float32 [2048], P('head')
- grad_proj_out: float32 [2048, 1024], P('head')
Inputs may be any that keep to these rules, and one draw needn't show every extreme that they name: `doc_start`: position 0 of every sequence is a document start. One sequence, drawn from the seed, holds a single document; the others may have further starts.
All inputs are finite; a program needn't handle non-finite values.
Results may differ from a plain program's by a relative error of at most 0.0065.
The roundings to bfloat16 on the way count: a program that leaves them out, or rounds other values in their place, can miss the bound.
Values may be sent and summed in bfloat16 or wider, within the bound.
No kernel may reach another device: no remote copies, remote signals or barrier semaphores. Data moves between devices by JAX's collectives and lax.ppermute only.
A program may use at most 256 MiB of HBM per device.

v0:
```python
from functools import partial

import jax
import jax.numpy as jnp
from jax import lax
from jax.sharding import PartitionSpec as P

EPS = 1e-05
HIGHEST = lax.Precision.HIGHEST


def passed_along(shard, axis, by):
    peers = lax.axis_size(axis)
    pairs = [(i, i + by) for i in range(peers) if 0 <= i + by < peers]
    return lax.ppermute(shard, axis, pairs)


def prefix(part, axis, combine, identity, reverse):
    count = lax.axis_size(axis)
    place = lax.axis_index(axis)
    ahead = count - 1 - place if reverse else place
    gathered = jax.tree.map(lambda a: lax.all_gather(a, axis), part)
    state = jax.tree.map(lambda a, e: jnp.zeros_like(a) + jnp.asarray(e, a.dtype), part, identity)

    def one(turn, state):
        source = count - 1 - turn if reverse else turn
        return combine(
            state, jax.tree.map(lambda a: lax.dynamic_index_in_dim(a, source, 0, False), gathered)
        )

    return lax.fori_loop(0, ahead, one, state)


def silu_slope(source):
    sigmoid = jax.nn.sigmoid(source)
    return sigmoid * (1.0 + source * (1.0 - sigmoid))


def compose(earlier, later):
    state_first, decay_first = earlier
    state_next, decay_next = later
    return (decay_next[..., None, None] * state_first + state_next, decay_first * decay_next)


def convolve(extended, kernel, kernel_bias, valid_taps):
    block_len = valid_taps.shape[2]
    summed = kernel_bias
    for offset in range(kernel.shape[0]):
        summed = (
            summed
            + kernel[offset]
            * extended[:, offset : offset + block_len]
            * valid_taps[offset][..., None]
        )
    return jax.nn.silu(summed)


def decays(step_pre, decay_log, scores, same_doc, fresh_rows, tail_same):
    step_size = jax.nn.softplus(step_pre)
    decay_rate = -jnp.exp(decay_log)
    cumlog = jnp.transpose(jnp.cumsum(step_size * decay_rate, axis=1), (0, 2, 1))
    step_heads = jnp.transpose(step_size, (0, 2, 1))
    spread = cumlog[..., :, None] - cumlog[..., None, :]
    keep_mask = same_doc[:, None]
    weights = (
        jnp.where(keep_mask, jnp.exp(jnp.where(keep_mask, spread, 0.0)), 0.0)
        * scores[:, None]
        * step_heads[:, :, None, :]
    )
    end_weight = jnp.exp(cumlog[..., -1:] - cumlog) * tail_same[:, None] * step_heads
    carry_decay = jnp.exp(cumlog[..., -1]) * fresh_rows[:, -1:]
    entry_decay = jnp.transpose(jnp.exp(cumlog), (0, 2, 1)) * fresh_rows[..., None]
    return (weights, end_weight, carry_decay, entry_decay)


def shards(
    hidden_in,
    doc_start,
    norm_gain,
    proj_gate,
    proj_value,
    proj_maps,
    proj_step,
    conv_value,
    value_bias,
    conv_maps,
    maps_bias,
    step_bias,
    decay_log,
    skip_gain,
    gate_gain,
    proj_out,
    out_grad,
):
    hidden_full, gain_full, grad_full = (
        lax.all_gather(hidden_in, "head", axis=2, tiled=True),
        lax.all_gather(norm_gain, "head", axis=0, tiled=True),
        lax.all_gather(out_grad, "head", axis=2, tiled=True),
    )
    seq_count, block_len, model_width = hidden_full.shape
    inner_loc = proj_value.shape[1]
    head_count = proj_step.shape[1]
    head_size = inner_loc // head_count
    kernel_len = conv_value.shape[0]
    head_devices = lax.axis_size("head")
    inner_all = inner_loc * head_devices
    residual = hidden_full.astype(jnp.float32)
    inv_norm = lax.rsqrt(jnp.mean(residual * residual, axis=-1, keepdims=True) + EPS)
    normed = (residual * inv_norm * gain_full.astype(jnp.float32)).astype(jnp.bfloat16)
    gate_pre = jnp.dot(normed, proj_gate, preferred_element_type=jnp.float32)
    value_pre = jnp.dot(normed, proj_value, preferred_element_type=jnp.float32).astype(jnp.bfloat16)
    maps_pre = jnp.dot(normed, proj_maps, preferred_element_type=jnp.float32).astype(jnp.bfloat16)
    step_pre = jnp.dot(normed, proj_step, preferred_element_type=jnp.float32) + step_bias
    mixed = jnp.concatenate([value_pre, maps_pre], axis=-1)
    kernel = jnp.concatenate([conv_value, conv_maps], axis=1)
    kernel_bias = jnp.concatenate([value_bias, maps_bias], axis=0)
    segment = jnp.cumsum(doc_start, axis=1)
    tail_starts = doc_start[:, block_len - (kernel_len - 1) :]
    after_tail = jnp.cumsum(tail_starts[:, ::-1], axis=1)[:, ::-1] - tail_starts
    tail_keep = (after_tail == 0).astype(jnp.bfloat16)[..., None]
    tail_rows = mixed[:, block_len - (kernel_len - 1) :] * tail_keep
    prior_rows = passed_along(tail_rows, "seq", 1)
    extended = jnp.concatenate([prior_rows, mixed], axis=1).astype(jnp.float32)
    segment_ext = jnp.concatenate(
        [jnp.zeros((seq_count, kernel_len - 1), jnp.int32), segment], axis=1
    )
    valid_taps = jnp.stack(
        [segment_ext[:, offset : offset + block_len] == segment for offset in range(kernel_len)],
        axis=0,
    ).astype(jnp.float32)
    activated, conv_back = jax.vjp(
        partial(convolve, valid_taps=valid_taps), extended, kernel, kernel_bias
    )
    values = activated[..., :inner_loc].astype(jnp.bfloat16)
    maps_local = activated[..., inner_loc:].astype(jnp.bfloat16)
    maps_all = lax.all_gather(maps_local, "head", axis=2, tiled=True)
    state_width = maps_all.shape[2] // 2
    write_map = maps_all[..., :state_width]
    read_map = maps_all[..., state_width:]
    causal = jnp.arange(block_len)[:, None] >= jnp.arange(block_len)[None, :]
    same_doc = causal[None] & (segment[:, :, None] == segment[:, None, :])
    fresh_rows = (segment == 0).astype(jnp.float32)
    tail_same = (segment == segment[:, -1:]).astype(jnp.float32)
    scores = jnp.einsum("stn,sqn->stq", read_map, write_map, preferred_element_type=jnp.float32)
    decay_parts = partial(decays, same_doc=same_doc, fresh_rows=fresh_rows, tail_same=tail_same)
    (weights, end_weight, carry_decay, entry_decay), decay_back = jax.vjp(
        decay_parts, step_pre, decay_log, scores
    )
    mixing = weights.astype(jnp.bfloat16)
    values_h = values.reshape(seq_count, block_len, head_count, head_size)
    diag_out = jnp.einsum("shtq,sqhp->sthp", mixing, values_h, preferred_element_type=jnp.float32)
    write_float = write_map.astype(jnp.float32)
    read_float = read_map.astype(jnp.float32)
    weighted = (end_weight[..., None] * write_float[:, None]).astype(jnp.bfloat16)
    local_state = jnp.einsum(
        "sqhp,shqn->shpn", values_h, weighted, preferred_element_type=jnp.float32
    )
    identity = (jnp.zeros_like(local_state), jnp.ones_like(carry_decay))
    incoming = prefix((local_state, carry_decay), "seq", compose, identity, False)[0]
    carried = jnp.einsum("stn,shpn->sthp", read_float, incoming, precision=HIGHEST)
    values_float = values_h.astype(jnp.float32)
    scan_out = diag_out + entry_decay[..., None] * carried + skip_gain[:, None] * values_float
    scan_flat = scan_out.reshape(seq_count, block_len, inner_loc)
    gate_act = jax.nn.silu(gate_pre)
    gate_prod = scan_flat * gate_act
    total_sq = lax.psum(jnp.sum(gate_prod * gate_prod, axis=-1), "head")
    inv_gate = lax.rsqrt(total_sq / inner_all + EPS)[..., None]
    gated_norm = gate_prod * inv_gate
    normed_out = (gated_norm * gate_gain).astype(jnp.bfloat16)
    partial_out = jnp.dot(normed_out, proj_out, preferred_element_type=jnp.float32)
    branch = lax.psum_scatter(partial_out, "head", scatter_dimension=2, tiled=True)
    hidden_loc = hidden_in.astype(jnp.float32)
    mixed_out = (hidden_loc + branch).astype(jnp.bfloat16)
    grad_proj_out = jnp.einsum(
        "sqi,sqd->id", normed_out, grad_full, preferred_element_type=jnp.float32
    )
    grad_normed = jnp.einsum("sqd,id->sqi", grad_full, proj_out, preferred_element_type=jnp.float32)
    grad_gate_gain = jnp.sum(grad_normed * gated_norm, axis=(0, 1))
    scaled = grad_normed * gate_gain
    inner_prod = lax.psum(jnp.sum(scaled * gate_prod, axis=-1), "head")
    grad_gated = (
        inv_gate * scaled
        - gate_prod * (inv_gate * inv_gate * inv_gate) * (inner_prod / inner_all)[..., None]
    )
    grad_scan = (
        (grad_gated * gate_act)
        .astype(jnp.bfloat16)
        .reshape(seq_count, block_len, head_count, head_size)
    )
    grad_gate_pre = (grad_gated * scan_flat * silu_slope(gate_pre)).astype(jnp.bfloat16)
    grad_scan_f = grad_scan.astype(jnp.float32)
    grad_skip = jnp.sum(grad_scan_f * values_float, axis=(0, 1, 3))
    grad_mixing = jnp.einsum(
        "sthp,sqhp->shtq", grad_scan, values_h, preferred_element_type=jnp.float32
    )
    grad_values = skip_gain[:, None] * grad_scan_f + jnp.einsum(
        "shtq,sthp->sqhp", mixing, grad_scan, preferred_element_type=jnp.float32
    )
    grad_entry = jnp.sum(grad_scan_f * carried, axis=-1)
    entry_grad = entry_decay[..., None] * grad_scan_f
    state_term = jnp.einsum("sthp,stn->shpn", entry_grad, read_float, precision=HIGHEST)
    grad_read = jnp.einsum("sthp,shpn->stn", entry_grad, incoming, precision=HIGHEST)
    outgoing = prefix((state_term, carry_decay), "seq", compose, identity, True)[0]
    grad_carry = jnp.sum(outgoing * incoming, axis=(2, 3))
    grad_values = grad_values + jnp.einsum(
        "shqn,shpn->sqhp", weighted.astype(jnp.float32), outgoing, precision=HIGHEST
    )
    grad_weighted = jnp.einsum("sqhp,shpn->shqn", values_float, outgoing, precision=HIGHEST)
    grad_end = jnp.sum(grad_weighted * write_float[:, None], axis=-1)
    grad_write = jnp.einsum("shqn,shq->sqn", grad_weighted, end_weight)
    grad_step, grad_decay_log, grad_scores = decay_back(
        (grad_mixing, grad_end, grad_carry, grad_entry)
    )
    grad_read = grad_read + jnp.einsum("stq,sqn->stn", grad_scores, write_float, precision=HIGHEST)
    grad_write = grad_write + jnp.einsum("stq,stn->sqn", grad_scores, read_float, precision=HIGHEST)
    grad_maps = lax.psum_scatter(
        jnp.concatenate([grad_write, grad_read], axis=-1), "head", scatter_dimension=2, tiled=True
    )
    grad_activated = jnp.concatenate(
        [grad_values.reshape(seq_count, block_len, inner_loc), grad_maps], axis=-1
    )
    grad_ext, grad_kernel, grad_kernel_bias = conv_back(grad_activated)
    head_rows = grad_ext[:, : kernel_len - 1]
    from_next = passed_along(head_rows, "seq", -1)
    grad_mixed = grad_ext[:, kernel_len - 1 :]
    grad_mixed = grad_mixed.at[:, block_len - (kernel_len - 1) :].add(
        from_next * tail_keep.astype(jnp.float32)
    )
    grad_value_pre = grad_mixed[..., :inner_loc].astype(jnp.bfloat16)
    grad_maps_pre = grad_mixed[..., inner_loc:].astype(jnp.bfloat16)
    grad_step_pre = grad_step.astype(jnp.bfloat16)
    grad_step_bias = jnp.sum(grad_step, axis=(0, 1))
    grad_proj_gate = jnp.einsum(
        "sqd,sqk->dk", normed, grad_gate_pre, preferred_element_type=jnp.float32
    )
    grad_proj_value = jnp.einsum(
        "sqd,sqk->dk", normed, grad_value_pre, preferred_element_type=jnp.float32
    )
    grad_proj_maps = jnp.einsum(
        "sqd,sqk->dk", normed, grad_maps_pre, preferred_element_type=jnp.float32
    )
    grad_proj_step = jnp.einsum(
        "sqd,sqk->dk", normed, grad_step_pre, preferred_element_type=jnp.float32
    )
    grad_in = jnp.einsum(
        "sqk,dk->sqd", grad_gate_pre, proj_gate, preferred_element_type=jnp.float32
    )
    grad_in = grad_in + jnp.einsum(
        "sqk,dk->sqd", grad_value_pre, proj_value, preferred_element_type=jnp.float32
    )
    grad_in = grad_in + jnp.einsum(
        "sqk,dk->sqd", grad_maps_pre, proj_maps, preferred_element_type=jnp.float32
    )
    grad_in = grad_in + jnp.einsum(
        "sqk,dk->sqd", grad_step_pre, proj_step, preferred_element_type=jnp.float32
    )
    row_part = jnp.sum(grad_in * gain_full.astype(jnp.float32) * residual, axis=-1)
    row_tiled = jnp.broadcast_to(row_part[..., None], (seq_count, block_len, head_devices))
    grad_in_loc, row_sum = (
        lax.psum_scatter(grad_in, "head", scatter_dimension=2, tiled=True),
        lax.psum_scatter(row_tiled, "head", scatter_dimension=2, tiled=True),
    )
    grad_norm_gain = jnp.sum(grad_in_loc * hidden_loc * inv_norm, axis=(0, 1))
    grad_normal = grad_in_loc * norm_gain.astype(jnp.float32)
    input_grad = (
        out_grad.astype(jnp.float32)
        + inv_norm * grad_normal
        - hidden_loc * (inv_norm * inv_norm * inv_norm) * (row_sum / model_width)
    )
    grad_conv_value = grad_kernel[:, :inner_loc]
    grad_conv_maps = grad_kernel[:, inner_loc:]
    grad_value_bias = grad_kernel_bias[:inner_loc]
    grad_maps_bias = grad_kernel_bias[inner_loc:]
    (
        grad_norm_gain,
        grad_proj_gate,
        grad_proj_value,
        grad_proj_maps,
        grad_proj_step,
        grad_conv_value,
        grad_value_bias,
        grad_conv_maps,
        grad_maps_bias,
        grad_step_bias,
        grad_decay_log,
        grad_skip,
        grad_gate_gain,
        grad_proj_out,
    ) = lax.psum(
        (
            grad_norm_gain,
            grad_proj_gate,
            grad_proj_value,
            grad_proj_maps,
            grad_proj_step,
            grad_conv_value,
            grad_value_bias,
            grad_conv_maps,
            grad_maps_bias,
            grad_step_bias,
            grad_decay_log,
            grad_skip,
            grad_gate_gain,
            grad_proj_out,
        ),
        "seq",
    )
    return (
        mixed_out,
        input_grad,
        grad_norm_gain,
        grad_proj_gate,
        grad_proj_value,
        grad_proj_maps,
        grad_proj_step,
        grad_conv_value,
        grad_value_bias,
        grad_conv_maps,
        grad_maps_bias,
        grad_step_bias,
        grad_decay_log,
        grad_skip,
        grad_gate_gain,
        grad_proj_out,
    )


def solution(mesh):
    placed = (
        P(None, "seq", "head"),
        P(None, "seq"),
        P("head"),
        P(None, "head"),
        P(None, "head"),
        P(None, "head"),
        P(None, "head"),
        P(None, "head"),
        P("head"),
        P(None, "head"),
        P("head"),
        P("head"),
        P("head"),
        P("head"),
        P("head"),
        P("head", None),
        P(None, "seq", "head"),
    )
    return jax.shard_map(
        shards,
        mesh=mesh,
        in_specs=placed,
        out_specs=(
            P(None, "seq", "head"),
            P(None, "seq", "head"),
            P("head"),
            P(None, "head"),
            P(None, "head"),
            P(None, "head"),
            P(None, "head"),
            P(None, "head"),
            P("head"),
            P(None, "head"),
            P("head"),
            P("head"),
            P("head"),
            P("head"),
            P("head"),
            P("head", None),
        ),
        check_vma=False,
    )
```

profile of v0, /device:TPU:0, one launch (start us, length us, event | category | flops | bytes accessed | tf_op | source)
XLA Modules:
  0.0 1012.7 jit_solution(17519539890220026369)
XLA Ops:
  15.9 1.9 all-gather.2
  18.2 3.1 all-gather.8.cloned.1.call-done
  23.5 2.3 fusion.87
  31.6 3.6 collective-permute-start
  37.0 3.5 multiply_convert_fusion.6
  41.4 2.3 slice.201
  43.7 2.0 all_gather.32
  47.9 1.8 copy.184
  49.7 2.8 fusion.7
  56.5 42.8 %all_gather.33 = f32[16,2,16]{2,1,0:T(2,128)} all-gather(f32[1,2,16]{2,1,0:T(2,128)S(1)} %bitcast_multiply_fusion.1), channel_id=1, replica_groups=mesh['seq'=16,'head'=2] {'seq'}, dimensions={0}, use_global_device_ids=true | all-gather | bytes 2176 | tf_op jit(solution)/shard_map/all_gather | solution.py:22
  100.4 145.8 %all-gather.12.cloned.1.call-done = f32[32,16,64,128]{3,2,1,0:T(8,128)} async-done(((f32[2,16,64,128]{3,2,1,0:T(8,128)}), f32[32,16,64,128]{3,2,1,0:T(8,128)}) %all-gather.12.cloned.1.call-update) | async-done | bytes 16777232 | tf_op jit(solution)/shard_map/all_gather | solution.py:22
  247.7 4.2 fusion.27
  251.9 3.0 copy.186
  254.9 6.1 multiply_reduce_fusion.11
  261.0 3.1 psum.112
  265.4 5.9 multiply_reduce_fusion.8
  271.3 3.3 psum.113
  275.3 6.1 multiply_reduce_fusion.9
  281.4 2.3 copy.188
  283.7 3.4 fusion.9
  287.2 4.9 fusion.40
  292.1 7.9 fusion.3
  302.0 2.6 fusion.23
  304.6 204.1 %all-gather.14.cloned.1.call-done = f32[32,16,64,128]{3,2,1,0:T(8,128)} async-done(((f32[2,16,64,128]{3,2,1,0:T(8,128)}), f32[32,16,64,128]{3,2,1,0:T(8,128)}) %all-gather.14.cloned.1.call-update) | async-done | bytes 16777232 | tf_op jit(solution)/shard_map/all_gather | solution.py:22
  508.8 31.9 %while.28 = (s32[]{:T(128)}, f32[2,16,64,128]{3,2,1,0:T(8,128)S(1)}, s32[]{:T(128)}, f32[16,2,16]{2,1,0:T(2,128)}, f32[16,2,16,64,128]{4,3,2,1,0:T(8,128)}, /*index=5*/s32[]{:T(128)}, s32[]{:T(128)}, s32[]{:T(128)}, s32[]{:T(128)}) while((s32[]{:T(128)}, f32[2,16,64,128]{3,2,1,0:T(8,128)S(1)}, s32[]{:T(128)}, f32[16,2,16]{2,1,0:T(2,128)}, ...), condition=%wide.region_14.15_spmd, body=%wide.region_13.14_spmd.sunk | while | flops 524294 | bytes 3146267 | solution.py:31
  540.7 4.7 multiply_reduce_fusion.2
  545.4 1.9 copy.216
  549.0 1.8 pad_maximum_fusion.1
  551.1 2.1 fusion.18
  553.5 4.4 fusion.21
  557.9 5.3 fusion.4
  564.2 3.3 multiply_reduce_fusion.3
  568.1 5.0 reduce-window.26
  573.3 4.3 fusion.17
  577.6 3.1 copy.195
  581.0 4.5 multiply_reduce_fusion.7
  588.7 3.5 collective-permute-done.1
  597.1 2.1 fusion.15
  599.9 4.8 convolution_bitcast_fusion.2
  604.8 3.4 convolution_bitcast_fusion
  610.7 3.4 convolution_bitcast_fusion.1
  615.7 2.5 all-reduce.11
  618.9 3.3 fusion.45
  622.2 77.1 %all-reduce.12 = (f32[512]{0:T(512)}, f32[4,1024]{1,0:T(4,128)}, f32[1024]{0:T(1024)}, f32[4,128]{1,0:T(4,128)}, f32[128]{0:T(128)}, /*index=5*/f32[16]{0:T(128)}, f32[16]{0:T(128)}, f32[16]{0:T(128)}, f32[1024]{0:T(1024)}) all-reduce(f32[512]{0:T(512)S(1)} %get-tuple-element.227, ...), channel_id=1, replica_groups=mesh['seq'=16,'head'=2] {'seq'}, use_global_device_ids=true, to_apply=%region_30.31 | all-reduce | flops 7344 | bytes 58752 | tf_op jit(solution)/shard_map/psum | solution.py:289
  699.3 294.0 %all-reduce.16.cloned.1.call-done = (f32[1024,1024]{1,0:T(8,128)}, f32[1024,1024]{1,0:T(8,128)}, f32[1024,128]{1,0:T(8,128)}, f32[1024,16]{0,1:T(8,128)}, f32[1024,1024]{1,0:T(8,128)}) async-done(((f32[1024,1024]{1,0:T(8,128)}, f32[1024,1024]{1,0:T(8,128)}, f32[1024,128]{1,0:T(8,128)}, f32[1024,16]{0,1:T(8,128)}, f32[1024,1024]{1,0:T(8,128)}), (f32[1024,1024]{1,0:T(8,128)}, f32[1024,1024]{1,0:T(8,128)}, ...) | async-done | bytes 13172752 | tf_op jit(solution)/shard_map/psum | solution.py:289
  993.3 4.9 copy.282
  998.2 2.1 copy.283
  1002.3 2.1 copy.286
  (329 shorter events, 84.2 us)
Async XLA Ops:
  7.2 247.7 %copy-start = (bf16[1024,1024]{1,0:T(8,128)(2,1)S(1)}, bf16[1024,1024]{1,0:T(8,128)(2,1)}, u32[]{:S(2)}) copy-start(bf16[1024,1024]{1,0:T(8,128)(2,1)} %param.26) | copy-start | bytes 6291460
  7.2 14.1 %all-gather.8.cloned.1.call-start = ((), (), s32[]{:S(2)}) async-start(), calls=%async_computation.3 | async-start | bytes 1572864 | tf_op jit(solution)/shard_map/all_gather | solution.py:96
  7.9 238.2 %all-gather.12.cloned.1.call-start = ((), (), s32[]{:S(2)}) async-start(), calls=%async_computation.8 | async-start | bytes 17825792 | tf_op jit(solution)/shard_map/all_gather | solution.py:22
  10.1 20.1 %copy-start.81 = (f32[16]{0:T(128)}, f32[16]{0:T(128)S(1)}, u32[]{:S(2)}) copy-start(f32[16]{0:T(128)S(1)} %exponential_negate_fusion) | copy-start | bytes 196
  11.2 6.9 copy-start.56
  17.8 12.3 %copy-start.66 = (f32[2,1,512]{2,1,0:T(1,128)}, f32[2,1,512]{2,1,0:T(1,128)S(1)}, u32[]{:S(2)}) copy-start(f32[2,1,512]{2,1,0:T(1,128)S(1)} %convert_element_type.120) | copy-start | bytes 12292
  17.9 19.0 %copy-start.36 = (f32[1152]{0:T(1024)}, f32[1152]{0:T(1024)S(1)}, u32[]{:S(2)}) copy-start(f32[1152]{0:T(1024)S(1)} %get-tuple-element.175) | copy-start | bytes 13828
  17.9 19.0 %copy-start.38 = (f32[1152]{0:T(1024)}, f32[1152]{0:T(1024)S(1)}, u32[]{:S(2)}) copy-start(f32[1152]{0:T(1024)S(1)} %get-tuple-element.176) | copy-start | bytes 13828
  18.1 17.1 %copy-start.43 = (f32[2,256]{1,0:T(2,128)}, f32[2,256]{1,0:T(2,128)S(1)}, u32[]{:S(2)}) copy-start(f32[2,256]{1,0:T(2,128)S(1)} %get-tuple-element.242) | copy-start | bytes 6148
  18.1 17.1 %copy-start.63 = (f32[2,256]{1,0:T(2,128)}, f32[2,256]{1,0:T(2,128)S(1)}, u32[]{:S(2)}) copy-start(f32[2,256]{1,0:T(2,128)S(1)} %get-tuple-element.243) | copy-start | bytes 6148
  18.2 18.8 %copy-start.46 = (f32[2,256]{1,0:T(2,128)}, f32[2,256]{1,0:T(2,128)S(1)}, u32[]{:S(2)}) copy-start(f32[2,256]{1,0:T(2,128)S(1)} %get-tuple-element.234) | copy-start | bytes 6148
  18.2 18.8 %copy-start.48 = (f32[2,256]{1,0:T(2,128)}, f32[2,256]{1,0:T(2,128)S(1)}, u32[]{:S(2)}) copy-start(f32[2,256]{1,0:T(2,128)S(1)} %get-tuple-element.235) | copy-start | bytes 6148
  18.2 18.8 %copy-start.50 = (f32[2,256]{1,0:T(2,128)}, f32[2,256]{1,0:T(2,128)S(1)}, u32[]{:S(2)}) copy-start(f32[2,256]{1,0:T(2,128)S(1)} %get-tuple-element.236) | copy-start | bytes 6148
  18.2 18.8 %copy-start.52 = (f32[2,256]{1,0:T(2,128)}, f32[2,256]{1,0:T(2,128)S(1)}, u32[]{:S(2)}) copy-start(f32[2,256]{1,0:T(2,128)S(1)} %get-tuple-element.237) | copy-start | bytes 6148
  21.3 7.3 copy-start.7
  23.5 6.6 copy-start.69
  27.3 8.0 copy-start.40
  28.7 6.5 copy-start.61
  31.6 5.1 collective-permute-start
  47.1 5.4 copy-start.9
  52.5 212.9 %all-gather.10.cloned.1.call-start = ((), (), s32[]{:S(2)}) async-start(), calls=%async_computation.5 | async-start | bytes 1572864 | tf_op jit(solution)/shard_map/all_gather | solution.py:98
  53.3 455.4 %all-gather.14.cloned.1.call-start = ((), (), s32[]{:S(2)}) async-start(), calls=%async_computation.9 | async-start | bytes 17825792 | tf_op jit(solution)/shard_map/all_gather | solution.py:22
  54.2 192.0 %copy-start.83 = (f32[2]{0:T(128)}, f32[2]{0:T(128)S(1)}, u32[]{:S(2)}) copy-start(f32[2]{0:T(128)S(1)} %slice_reduce_fusion.9) | copy-start | bytes 28
  247.4 4.5 copy-start.6
  287.1 293.8 %reduce-scatter.6.cloned.1.call-start = ((), (), s32[]{:S(2)}) async-start(), calls=%async_computation.6 | async-start | bytes 786432 | tf_op jit(solution)/shard_map/reduce_scatter | solution.py:216
  287.2 4.9 copy-start.4
  287.2 4.9 copy-start.11
  287.2 4.9 copy-start.30
  287.2 4.9 copy-start.34
  287.2 4.9 copy-start.58
  292.1 9.8 copy-start.24
  508.8 31.9 %copy-start.12 = (bf16[2,256,1024]{1,2,0:T(8,128)(2,1)S(1)}, bf16[2,256,1024]{1,2,0:T(8,128)(2,1)}, u32[]{:S(2)}) copy-start(bf16[2,256,1024]{1,2,0:T(8,128)(2,1)} %copy-done.9) | copy-start | bytes 3145732
  545.4 5.7 copy-start.5
  550.8 68.0 %reduce-scatter.4.cloned.1.call-start = ((), (), s32[]{:S(2)}) async-start(), calls=%async_computation.4 | async-start | bytes 3145728 | tf_op jit(solution)/shard_map/reduce_scatter | solution.py:171
  563.2 55.7 %reduce-scatter.8.cloned.1.call-start = ((), (), s32[]{:S(2)}) async-start(), calls=%async_computation.7 | async-start | bytes 3145728 | tf_op jit(solution)/shard_map/reduce_scatter | solution.py:260
  564.2 9.1 copy-start.86
  581.0 4.5 copy-start.37
  581.0 4.5 copy-start.39
  586.4 5.9 collective-permute-start.1
  599.3 5.5 copy-start.17
  599.3 5.5 copy-start.72
  599.3 5.5 copy-start.74
  599.3 394.0 %all-reduce.16.cloned.1.call-start = ((), (), s32[]{:S(2)}) async-start(), calls=%async_computation.10 | async-start | bytes 26345472 | tf_op jit(solution)/shard_map/psum | solution.py:289
  599.9 4.8 copy-start.89
  614.1 4.8 copy-start.19
  614.1 4.8 copy-start.20
  614.1 4.8 copy-start.68
  993.3 4.9 copy-start.14
  (54 other events, 141.8 us)
Sparse Core Ops, SparseCore 0:
  9.6 11.7 all-gather.7
  52.6 193.4 all-gather.11
  247.7 7.2 all-gather.9
  287.2 221.3 all-gather.13
  550.9 3.8 reduce-scatter.5
  563.3 5.4 reduce-scatter.3
  599.4 5.4 reduce-scatter.7
  614.2 378.9 all-reduce.15
where the time goes:
time: 1020 us; the launch traced here: 1010 us
  waiting for transfers between devices  653 us (64%)
  blocking collectives  133 us (13%)
  matrix products  84.2 us (8%)
  other arithmetic  68.7 us (7%)
  local copies, waits for them, and re-layouts  52.5 us (5%)
  between operations  15.7 us (2%)
    all_gather x2, waiting for transfers between devices, prefix(): gathered = jax.tree.map(lambda a: lax.all_gather(a, axis), part)  350 us
    psum x1, waiting for transfers between devices, shards(): lax.psum((grad_norm_gain, grad_proj_gate, grad_proj_value, grad_proj_maps...  294 us
    psum x1, blocking collectives, shards(): lax.psum((grad_norm_gain, grad_proj_gate, grad_proj_value, grad_proj_maps...  77.1 us
    all_gather x1, blocking collectives, prefix(): gathered = jax.tree.map(lambda a: lax.all_gather(a, axis), part)  42.8 us
    add x15, other arithmetic, compose(): decay_next[..., None, None] * state_first + state_next  21.6 us
  transfers between devices with their start and end apart: 10, of which 6 were waited for; matrix products, arithmetic and copies ran while one was open for 10% of the time, Pallas kernels for 0%

commit v1 on v0

--- a/solution.py
+++ b/solution.py
@@ -15,31 +15,96 @@
     return lax.ppermute(shard, axis, pairs)
 
 
-def prefix(part, axis, combine, identity, reverse):
+def scan_rows(states, decay_rows, reverse):
+    count = states.shape[0]
+    order = range(count - 1, -1, -1) if reverse else range(count)
+    carried = jnp.zeros_like(states[0])
+    entering = [None] * count
+    for block in order:
+        entering[block] = carried
+        carried = decay_rows[block][:, None] * carried + states[block]
+    return jnp.stack(entering, axis=0)
+
+
+def exchange_scan(state, decay_rows, axis, reverse):
+    count = lax.axis_size(axis)
+    width = state.shape[-1]
+    rows = state.reshape(count, -1, width)
+    spread = lax.all_to_all(rows, axis, 0, 0, tiled=True)
+    entering = scan_rows(spread, decay_rows, reverse)
+    back = lax.all_to_all(entering, axis, 0, 0, tiled=True)
+    return back.reshape(state.shape)
+
+
+def flip(shard, axis, mask):
+    count = lax.axis_size(axis)
+    return lax.ppermute(shard, axis, [(i, i ^ mask) for i in range(count)])
+
+
+def stages(count):
+    bits = count.bit_length() - 1
+    groups = []
+    bit = 0
+    while bit < bits:
+        take = 2 if bit >= 2 and bit + 2 <= bits else 1
+        groups.append((bit, take))
+        bit += take
+    return groups
+
+
+def reduce_all(part, axis, order, first_low=True):
     count = lax.axis_size(axis)
     place = lax.axis_index(axis)
-    ahead = count - 1 - place if reverse else place
-    gathered = jax.tree.map(lambda a: lax.all_gather(a, axis), part)
-    state = jax.tree.map(lambda a, e: jnp.zeros_like(a) + jnp.asarray(e, a.dtype), part, identity)
-
-    def one(turn, state):
-        source = count - 1 - turn if reverse else turn
-        return combine(
-            state, jax.tree.map(lambda a: lax.dynamic_index_in_dim(a, source, 0, False), gathered)
-        )
-
-    return lax.fori_loop(0, ahead, one, state)
+    groups = [stages(count)[i] for i in order]
+    acc = part
+    for turn, (bit, take) in enumerate(groups):
+        ways = 1 << take
+        piece = acc.shape[0] // ways
+        mine = (place >> bit) & (ways - 1)
+        kept = lax.dynamic_slice_in_dim(acc, mine * piece, piece, 0)
+        for step in range(1, ways):
+            sent = lax.dynamic_slice_in_dim(acc, (mine ^ step) * piece, piece, 0)
+            if turn == 0 and first_low:
+                got = flip(sent.astype(jnp.bfloat16), axis, step << bit).astype(jnp.float32)
+            else:
+                got = flip(sent, axis, step << bit)
+            kept = kept + got
+        acc = kept
+    acc = acc.astype(jnp.bfloat16)
+    for bit, take in reversed(groups):
+        ways = 1 << take
+        piece = acc.shape[0]
+        mine = (place >> bit) & (ways - 1)
+        whole = jnp.zeros((piece * ways,) + acc.shape[1:], acc.dtype)
+        whole = lax.dynamic_update_slice_in_dim(whole, acc, mine * piece, 0)
+        for step in range(1, ways):
+            got = flip(acc, axis, step << bit)
+            whole = lax.dynamic_update_slice_in_dim(whole, got, (mine ^ step) * piece, 0)
+        acc = whole
+    return acc.astype(jnp.float32)
+
+
+def sum_weight(part, axis):
+    half = part.shape[0] // 2
+    orders = list(range(len(stages(lax.axis_size(axis)))))
+    other = [orders[1], orders[0]] + orders[2:]
+    return jnp.concatenate(
+        [reduce_all(part[:half], axis, orders), reduce_all(part[half:], axis, other)], axis=0
+    )
+
+
+def sum_small(part, axis):
+    count = lax.axis_size(axis)
+    mask = 1
+    while mask < count:
+        part = part + flip(part, axis, mask)
+        mask *= 2
+    return part
 
 
 def silu_slope(source):
     sigmoid = jax.nn.sigmoid(source)
     return sigmoid * (1.0 + source * (1.0 - sigmoid))
-
-
-def compose(earlier, later):
-    state_first, decay_first = earlier
-    state_next, decay_next = later
-    return (decay_next[..., None, None] * state_first + state_next, decay_first * decay_next)
 
 
 def convolve(extended, kernel, kernel_bias, valid_taps):
@@ -99,6 +164,7 @@
     )
     seq_count, block_len, model_width = hidden_full.shape
     inner_loc = proj_value.shape[1]
+    inner_maps = proj_maps.shape[1]
     head_count = proj_step.shape[1]
     head_size = inner_loc // head_count
     kernel_len = conv_value.shape[0]
@@ -155,8 +221,12 @@
     local_state = jnp.einsum(
         "sqhp,shqn->shpn", values_h, weighted, preferred_element_type=jnp.float32
     )
-    identity = (jnp.zeros_like(local_state), jnp.ones_like(carry_decay))
-    incoming = prefix((local_state, carry_decay), "seq", compose, identity, False)[0]
+    decay_all = lax.all_gather(carry_decay.reshape(-1), "seq")
+    row_count = seq_count * head_count * head_size
+    row_decay = jnp.repeat(decay_all, head_size, axis=1)
+    share = row_count // lax.axis_size("seq")
+    row_decay = lax.dynamic_slice_in_dim(row_decay, lax.axis_index("seq") * share, share, 1)
+    incoming = exchange_scan(local_state, row_decay, "seq", False)
     carried = jnp.einsum("stn,shpn->sthp", read_float, incoming, precision=HIGHEST)
     values_float = values_h.astype(jnp.float32)
     scan_out = diag_out + entry_decay[..., None] * carried + skip_gain[:, None] * values_float
@@ -200,7 +270,7 @@
     entry_grad = entry_decay[..., None] * grad_scan_f
     state_term = jnp.einsum("sthp,stn->shpn", entry_grad, read_float, precision=HIGHEST)
     grad_read = jnp.einsum("sthp,shpn->stn", entry_grad, incoming, precision=HIGHEST)
-    outgoing = prefix((state_term, carry_decay), "seq", compose, identity, True)[0]
+    outgoing = exchange_scan(state_term, row_decay, "seq", True)
     grad_carry = jnp.sum(outgoing * incoming, axis=(2, 3))
     grad_values = grad_values + jnp.einsum(
         "shqn,shpn->sqhp", weighted.astype(jnp.float32), outgoing, precision=HIGHEST
@@ -271,12 +341,18 @@
     grad_conv_maps = grad_kernel[:, inner_loc:]
     grad_value_bias = grad_kernel_bias[:inner_loc]
     grad_maps_bias = grad_kernel_bias[inner_loc:]
-    (
+    grad_proj_gate = sum_weight(grad_proj_gate, "seq")
+    grad_proj_value = sum_weight(grad_proj_value, "seq")
+    grad_proj_out = sum_weight(grad_proj_out, "seq")
+    lanes = 128
+    wide = jnp.concatenate([grad_proj_maps, grad_proj_step], axis=1)
+    wide = jnp.pad(wide, ((0, 0), (0, -wide.shape[1] % lanes)))
+    wide = reduce_all(wide, "seq", list(range(len(stages(lax.axis_size("seq"))))), False)
+    grad_proj_maps, grad_proj_step = jnp.split(
+        wide[:, : inner_maps + head_count], [inner_maps], axis=1
+    )
+    smalls = [
         grad_norm_gain,
-        grad_proj_gate,
-        grad_proj_value,
-        grad_proj_maps,
-        grad_proj_step,
         grad_conv_value,
         grad_value_bias,
         grad_conv_maps,
@@ -285,26 +361,25 @@
         grad_decay_log,
         grad_skip,
         grad_gate_gain,
-        grad_proj_out,
-    ) = lax.psum(
-        (
-            grad_norm_gain,
-            grad_proj_gate,
-            grad_proj_value,
-            grad_proj_maps,
-            grad_proj_step,
-            grad_conv_value,
-            grad_value_bias,
-            grad_conv_maps,
-            grad_maps_bias,
-            grad_step_bias,
-            grad_decay_log,
-            grad_skip,
-            grad_gate_gain,
-            grad_proj_out,
-        ),
-        "seq",
-    )
+    ]
+    flat = jnp.concatenate([a.reshape(-1) for a in smalls])
+    flat = jnp.pad(flat, (0, -flat.shape[0] % (8 * lanes))).reshape(-1, lanes)
+    flat = sum_small(flat, "seq").reshape(-1)
+    found, start = [], 0
+    for a in smalls:
+        found.append(flat[start : start + a.size].reshape(a.shape))
+        start += a.size
+    (
+        grad_norm_gain,
+        grad_conv_value,
+        grad_value_bias,
+        grad_conv_maps,
+        grad_maps_bias,
+        grad_step_bias,
+        grad_decay_log,
+        grad_skip,
+        grad_gate_gain,
+    ) = found
     return (
         mixed_out,
         input_grad,

time: 1020 us -> 606 us (0.59)
  waiting for transfers between devices: 653 us -> 124 us
  starting transfers between devices: 5.7 us -> 143 us
  blocking collectives: 133 us -> 62.4 us
  other arithmetic: 68.7 us -> 102 us
  local copies, waits for them, and re-layouts: 52.5 us -> 67.5 us
    all_gather x2 -> x0, waiting for transfers between devices: 350 us -> none  [prefix(): gathered = jax.tree.map(lambda a: lax.all_gather(a, axis), part)]
    psum x1 -> x0, waiting for transfers between devices: 294 us -> none  [shards(): lax.psum((grad_norm_gain, grad_proj_gate, grad_proj_value, grad_proj_maps...]
    ppermute x0 -> x74, starting transfers between devices: none -> 115 us  [flip(): return lax.ppermute(shard, axis, [(i, i ^ mask) for i in range(count)])]
    ppermute x0 -> x74, waiting for transfers between devices: none -> 86.4 us  [flip(): return lax.ppermute(shard, axis, [(i, i ^ mask) for i in range(count)])]
    psum x1 -> x0, blocking collectives: 77.1 us -> none  [shards(): lax.psum((grad_norm_gain, grad_proj_gate, grad_proj_value, grad_proj_maps...]
    unnamed x1 -> x24, other arithmetic: 0.07 us -> 34.4 us
    all_to_all x0 -> x4, waiting for transfers between devices: none -> 30.3 us  [the longest x2 19.7 us: exchange_scan(): back = lax.all_to_all(entering, axis, 0, 0, tiled=True)]
    all_to_all x0 -> x4, starting transfers between devices: none -> 22.3 us  [the longest x2 12.1 us: exchange_scan(): spread = lax.all_to_all(rows, axis, 0, 0, tiled=True)]
  transfers between devices with their start and end apart: 10 -> 85, of which waited for: 6 -> 33; matrix products, arithmetic and copies ran while one was open for 10% -> 30% of each run, Pallas kernels for 0% -> 0%
where the time goes in v1:
time: 606 us; the launch traced here: 595 us
  starting transfers between devices  143 us (24%)
  waiting for transfers between devices  124 us (20%)
  other arithmetic  102 us (17%)
  matrix products  79.1 us (13%)
  local copies, waits for them, and re-layouts  67.5 us (11%)
  blocking collectives  62.4 us (10%)
  between operations  16.9 us (3%)
    ppermute x74, starting transfers between devices, flip(): return lax.ppermute(shard, axis, [(i, i ^ mask) for i in range(count)])  115 us
    ppermute x74, waiting for transfers between devices, flip(): return lax.ppermute(shard, axis, [(i, i ^ mask) for i in range(count)])  86.4 us
    all_gather x1, blocking collectives, shards(): decay_all = lax.all_gather(carry_decay.reshape(-1), 'seq')  49.9 us
    unnamed x24, other arithmetic  34.4 us
    all_to_all x2, waiting for transfers between devices, exchange_scan(): back = lax.all_to_all(entering, axis, 0, 0, tiled=True)  19.7 us
    unnamed x309, local copies, waits for them, and re-layouts  16.7 us
  transfers between devices with their start and end apart: 85, of which 33 were waited for; matrix products, arithmetic and copies ran while one was open for 30% of the time, Pallas kernels for 0%

profile of v1, /device:TPU:0, one launch (start us, length us, event | category | flops | bytes accessed | tf_op | source)
XLA Modules:
  0.0 594.5 jit_solution(4471824507717690704)
XLA Ops:
  31.4 3.7 collective-permute-start
  51.2 7.3 %all-to-all-start = ((f32[16,128,128]{2,1,0:T(8,128)}), f32[16,128,128]{2,1,0:T(8,128)S(1)}, u32[]{:S(2)}, u32[]{:S(2)}) async-start(f32[16,128,128]{2,1,0:T(8,128)} %bitcast.301), calls=%async_computation | async-start | bytes 2097152 | tf_op jit(solution)/shard_map/all_to_all | solution.py:33
  59.6 49.9 %all-gather.1 = f32[16,1,32]{2,1,0:T(1,128)S(1)} all-gather(f32[1,1,32]{2,1,0:T(1,128)S(1)} %multiply_bitcast_fusion.2), channel_id=1, replica_groups=mesh['seq'=16,'head'=2] {'seq'}, dimensions={0}, use_global_device_ids=true | all-gather | bytes 2176 | tf_op jit(solution)/shard_map/all_gather | solution.py:224
  136.9 3.7 all-to-all-start.1
  143.2 16.2 %all-to-all-done.1 = f32[16,128,128]{2,1,0:T(8,128)S(1)} async-done(((f32[16,128,128]{2,1,0:T(8,128)}), f32[16,128,128]{2,1,0:T(8,128)S(1)}, u32[]{:S(2)}, u32[]{:S(2)}) %all-to-all-start.1) | async-done | bytes 1048608 | tf_op jit(solution)/shard_map/all_to_all | solution.py:35
  161.2 4.2 fusion.27
  168.4 5.1 multiply_reduce_fusion.11
  176.2 6.1 %multiply_reduce_fusion.8 = (f32[1024]{0:T(1024)}, f32[2,256]{1,0:T(2,128)}, f32[2,256,1024]{2,1,0:T(8,128)}) fusion(f32[2,256,1024]{2,1,0:T(8,128)} %get-tuple-element.171, f32[2,256]{1,0:T(2,128)S(1)} %get-tuple-element.255, f32[1024]{0:T(1024)} %param.33, bf16[2,256,1024]{2,1,0:T(8,128)(2,1)} %all-gather.7.cloned.1.call-done, bf16[1024,1024]{1,0:T(8,128)(2,1)} %param.34), kind=kOutput, calls=%fused_computation.67 | convolution fusion | flops 1076886016 | bytes 7352320 | tf_op jit(solution)/shard_map/sqd,id->sqi/dot_general | solution.py:247
  186.1 5.8 multiply_reduce_fusion.9
  195.6 4.8 all-to-all-start.2
  211.1 3.4 convolution_bitcast_fusion
  214.5 10.5 %all-to-all-done.2 = f32[16,128,128]{2,1,0:T(8,128)} async-done(((f32[16,128,128]{2,1,0:T(8,128)}), f32[16,128,128]{2,1,0:T(8,128)}, u32[]{:S(2)}, u32[]{:S(2)}) %all-to-all-start.2) | async-done | bytes 1048608 | tf_op jit(solution)/shard_map/all_to_all | solution.py:33
  243.3 6.5 %all-to-all-start.3 = ((f32[16,128,128]{2,1,0:T(8,128)}), f32[16,128,128]{2,1,0:T(8,128)}, u32[]{:S(2)}, u32[]{:S(2)}) async-start(f32[16,128,128]{2,1,0:T(8,128)} %constant_dynamic-update-slice_fusion.18), calls=%async_computation.4 | async-start | bytes 2097152 | tf_op jit(solution)/shard_map/all_to_all | solution.py:35
  250.3 4.1 fusion.112
  257.2 3.5 fusion.40
  260.8 6.9 %fusion.3 = (f32[2,16,256]{2,1,0:T(8,128)}, f32[2,16,256]{2,1,0:T(8,128)}, f32[2,16,256]{2,1,0:T(8,128)}, f32[2,256,256]{2,1,0:T(8,128)S(1)}) fusion(f32[2,16,256]{2,1,0:T(8,128)S(1)} %copy-done.88, f32[2,256,256]{2,1,0:T(8,128)S(1)} %copy-done.45, f32[2,16,256]{2,1,0:T(8,128)S(1)} %copy-done.56, pred[2,256,256]{2,1,0:T(8,128)(4,1)S(1)} %copy-done.58, ...), kind=kOutput, calls=%fused_computation.8 | convolution fusion | flops 299737088 | bytes 3440640 | tf_op jit(solution)/shard_map/sthp,sqhp->shtq/dot_general | solution.py:263
  269.6 3.5 all-to-all-done.3
  273.1 6.2 %multiply_reduce_fusion.2 = (f32[2,256,128]{1,2,0:T(8,128)}, f32[2,16,256,128]{2,3,1,0:T(8,128)}) fusion(f32[2,256,16]{1,2,0:T(8,128)S(1)} %bitcast.302, bf16[2,256,16,64]{1,3,2,0:T(8,128)(2,1)} %bitcast.296, f32[2,16,64,128]{3,2,1,0:T(8,128)} %bitcast.46), kind=kOutput, calls=%fused_computation.9 | convolution fusion | flops 807337984 | bytes 6586368 | tf_op jit(solution)/shard_map/sqhp,shpn->shqn/dot_general | solution.py:278
  287.4 4.9 fusion.21
  292.4 5.3 fusion.4
  297.9 4.0 fusion.23
  313.6 6.1 %collective-permute-done.17 = f32[128,1024]{1,0:T(8,128)S(1)} collective-permute-done((f32[128,1024]{1,0:T(8,128)S(1)}, f32[128,1024]{1,0:T(8,128)S(1)}, u32[]{:S(2)}, u32[]{:S(2)}) %collective-permute-start.17) | collective-permute-done | bytes 524320 | tf_op jit(solution)/shard_map/ppermute | solution.py:41
  326.7 3.7 collective-permute-start.10
  330.4 4.2 collective-permute-start.9
  339.3 5.4 collective-permute-start.68
  344.7 5.2 collective-permute-done.9
  349.9 4.7 collective-permute-start.60
  355.3 3.6 collective-permute-done.69
  359.0 5.2 collective-permute-start.22
  364.3 3.9 collective-permute-done.59
  368.2 3.9 collective-permute-start.12
  372.9 3.9 collective-permute-start.72
  379.0 4.6 collective-permute-start.62
  384.9 3.4 collective-permute-start.14
  390.2 3.4 collective-permute-done.24
  403.5 7.5 %collective-permute-done.25 = bf16[256,1024]{1,0:T(8,128)(2,1)S(1)} collective-permute-done((bf16[256,1024]{1,0:T(8,128)(2,1)S(1)}, bf16[256,1024]{1,0:T(8,128)(2,1)S(1)}, u32[]{:S(2)}, u32[]{:S(2)}) %collective-permute-start.25) | collective-permute-done | bytes 524320 | tf_op jit(solution)/shard_map/ppermute | solution.py:41
  411.1 5.5 collective-permute-done.75
  426.3 5.2 reduce-window.26
  432.2 4.6 fusion.17
  444.4 4.5 multiply_reduce_fusion.7
  476.0 6.8 %collective-permute-done.46 = f32[512,256]{0,1:T(8,128)} collective-permute-done((f32[512,256]{0,1:T(8,128)}, f32[512,256]{0,1:T(8,128)}, u32[]{:S(2)}, u32[]{:S(2)}) %collective-permute-start.46) | collective-permute-done | bytes 524320 | tf_op jit(solution)/shard_map/ppermute | solution.py:41
  485.6 4.8 collective-permute-done.47
  490.6 3.9 collective-permute-start.50
  498.7 5.9 collective-permute-done.49
  505.7 3.4 collective-permute-start.52
  523.9 3.4 collective-permute-start.38
  532.1 5.5 collective-permute-done.39
  575.2 3.8 collective-permute-done.4
  (724 shorter events, 285.8 us)
Async XLA Ops:
  7.2 14.2 %all-gather.5.cloned.1.call-start = ((), (), s32[]{:S(2)}) async-start(), calls=%async_computation.7 | async-start | bytes 1572864 | tf_op jit(solution)/shard_map/all_gather | solution.py:161
  51.2 62.8 %all-to-all-start = ((f32[16,128,128]{2,1,0:T(8,128)}), f32[16,128,128]{2,1,0:T(8,128)S(1)}, u32[]{:S(2)}, u32[]{:S(2)}) async-start(f32[16,128,128]{2,1,0:T(8,128)} %bitcast.301), calls=%async_computation | async-start | bytes 2097152 | tf_op jit(solution)/shard_map/all_to_all | solution.py:33
  136.9 22.5 %all-to-all-start.1 = ((f32[16,128,128]{2,1,0:T(8,128)}), f32[16,128,128]{2,1,0:T(8,128)S(1)}, u32[]{:S(2)}, u32[]{:S(2)}) async-start(f32[16,128,128]{2,1,0:T(8,128)} %constant_dynamic-update-slice_fusion.2), calls=%async_computation.1 | async-start | bytes 2097152 | tf_op jit(solution)/shard_map/all_to_all | solution.py:35
  140.6 35.6 %all-gather.7.cloned.1.call-start = ((), (), s32[]{:S(2)}) async-start(), calls=%async_computation.9 | async-start | bytes 1572864 | tf_op jit(solution)/shard_map/all_gather | solution.py:163
  195.6 29.5 %all-to-all-start.2 = ((f32[16,128,128]{2,1,0:T(8,128)}), f32[16,128,128]{2,1,0:T(8,128)}, u32[]{:S(2)}, u32[]{:S(2)}) async-start(f32[16,128,128]{2,1,0:T(8,128)} %bitcast.299), calls=%async_computation.3 | async-start | bytes 2097152 | tf_op jit(solution)/shard_map/all_to_all | solution.py:33
  206.9 95.4 %collective-permute-start.16 = (bf16[256,1024]{1,0:T(8,128)(2,1)}, bf16[256,1024]{1,0:T(8,128)(2,1)}, u32[]{:S(2)}, u32[]{:S(2)}) collective-permute-start(bf16[256,1024]{1,0:T(8,128)(2,1)} %dynamic-slice_convert_fusion.4), channel_id=1, source_target_pairs={{0,4},{2,6},{4,0},{6,2},{8,12},{10,14},{12,8},{14,10},{16,20},{18,... | collective-permute-start | bytes 1572872 | tf_op jit(solution)/shard_map/ppermute | solution.py:41
  209.6 96.7 %collective-permute-start.6 = (bf16[256,1024]{1,0:T(8,128)(2,1)}, bf16[256,1024]{1,0:T(8,128)(2,1)}, u32[]{:S(2)}, u32[]{:S(2)}) collective-permute-start(bf16[256,1024]{1,0:T(8,128)(2,1)} %dynamic-slice_convert_fusion.5), channel_id=1, source_target_pairs={{0,2},{2,0},{4,6},{6,4},{8,10},{10,8},{12,14},{14,12},{16,18},{18,... | collective-permute-start | bytes 1572872 | tf_op jit(solution)/shard_map/ppermute | solution.py:41
  243.3 29.8 %all-to-all-start.3 = ((f32[16,128,128]{2,1,0:T(8,128)}), f32[16,128,128]{2,1,0:T(8,128)}, u32[]{:S(2)}, u32[]{:S(2)}) async-start(f32[16,128,128]{2,1,0:T(8,128)} %constant_dynamic-update-slice_fusion.18), calls=%async_computation.4 | async-start | bytes 2097152 | tf_op jit(solution)/shard_map/all_to_all | solution.py:35
  249.8 194.5 %reduce-scatter.6.cloned.1.call-start = ((), (), s32[]{:S(2)}) async-start(), calls=%async_computation.10 | async-start | bytes 786432 | tf_op jit(solution)/shard_map/reduce_scatter | solution.py:286
  255.3 54.3 %collective-permute-start.66 = (bf16[256,1024]{1,0:T(8,128)(2,1)}, bf16[256,1024]{1,0:T(8,128)(2,1)}, u32[]{:S(2)}, u32[]{:S(2)}) collective-permute-start(bf16[256,1024]{1,0:T(8,128)(2,1)} %dynamic-slice_convert_fusion), channel_id=1, source_target_pairs={{0,4},{2,6},{4,0},{6,2},{8,12},{10,14},{12,8},{14,10},{16,20},{18,... | collective-permute-start | bytes 1572872 | tf_op jit(solution)/shard_map/ppermute | solution.py:41
  284.7 277.8 %reduce-scatter.4.cloned.1.call-start = ((), (), s32[]{:S(2)}) async-start(), calls=%async_computation.8 | async-start | bytes 3145728 | tf_op jit(solution)/shard_map/reduce_scatter | solution.py:241
  286.9 24.7 %collective-permute-start.56 = (bf16[256,1024]{1,0:T(8,128)(2,1)}, bf16[256,1024]{1,0:T(8,128)(2,1)}, u32[]{:S(2)}, u32[]{:S(2)}) collective-permute-start(bf16[256,1024]{1,0:T(8,128)(2,1)} %dynamic-slice_convert_fusion.1), channel_id=1, source_target_pairs={{0,2},{2,0},{4,6},{6,4},{8,10},{10,8},{12,14},{14,12},{16,18},{18,... | collective-permute-start | bytes 1572872 | tf_op jit(solution)/shard_map/ppermute | solution.py:41
  297.7 264.9 %reduce-scatter.8.cloned.1.call-start = ((), (), s32[]{:S(2)}) async-start(), calls=%async_computation.11 | async-start | bytes 3145728 | tf_op jit(solution)/shard_map/reduce_scatter | solution.py:330
  304.8 14.9 %collective-permute-start.17 = (f32[128,1024]{1,0:T(8,128)S(1)}, f32[128,1024]{1,0:T(8,128)S(1)}, u32[]{:S(2)}, u32[]{:S(2)}) collective-permute-start(f32[128,1024]{1,0:T(8,128)S(1)} %constant_dynamic-slice_fusion.25), channel_id=1, source_target_pairs={{0,2},{2,0},{4,6},{6,4},{8,10},{10,8},{12,14},{14,12},{16,18},{18,... | collective-permute-start | bytes 1572872 | tf_op jit(solution)/shard_map/ppermute | solution.py:41
  307.6 17.1 %collective-permute-start.7 = (f32[128,1024]{1,0:T(8,128)S(1)}, f32[128,1024]{1,0:T(8,128)S(1)}, u32[]{:S(2)}, u32[]{:S(2)}) collective-permute-start(f32[128,1024]{1,0:T(8,128)S(1)} %constant_dynamic-slice_fusion.29), channel_id=1, source_target_pairs={{0,4},{2,6},{4,0},{6,2},{8,12},{10,14},{12,8},{14,10},{16,20},{18,... | collective-permute-start | bytes 1572872 | tf_op jit(solution)/shard_map/ppermute | solution.py:41
  310.9 15.7 %collective-permute-start.67 = (f32[128,1024]{1,0:T(8,128)S(1)}, f32[128,1024]{1,0:T(8,128)S(1)}, u32[]{:S(2)}, u32[]{:S(2)}) collective-permute-start(f32[128,1024]{1,0:T(8,128)S(1)} %constant_dynamic-slice_fusion.4), channel_id=1, source_target_pairs={{0,2},{2,0},{4,6},{6,4},{8,10},{10,8},{12,14},{14,12},{16,18},{18,... | collective-permute-start | bytes 1572872 | tf_op jit(solution)/shard_map/ppermute | solution.py:41
  312.9 17.5 %collective-permute-start.57 = (f32[128,1024]{1,0:T(8,128)S(1)}, f32[128,1024]{1,0:T(8,128)S(1)}, u32[]{:S(2)}, u32[]{:S(2)}) collective-permute-start(f32[128,1024]{1,0:T(8,128)S(1)} %constant_dynamic-slice_fusion.8), channel_id=1, source_target_pairs={{0,4},{2,6},{4,0},{6,2},{8,12},{10,14},{12,8},{14,10},{16,20},{18,... | collective-permute-start | bytes 1572872 | tf_op jit(solution)/shard_map/ppermute | solution.py:41
  319.8 15.0 %collective-permute-start.20 = (f32[32,1024]{1,0:T(8,128)S(1)}, f32[32,1024]{1,0:T(8,128)S(1)}, u32[]{:S(2)}, u32[]{:S(2)}) collective-permute-start(f32[32,1024]{1,0:T(8,128)S(1)} %get-tuple-element.217), channel_id=1, source_target_pairs={{0,24},{2,26},{4,28},{6,30},{8,16},{10,18},{12,20},{14,22},{16,8},... | collective-permute-start | bytes 393224 | tf_op jit(solution)/shard_map/ppermute | solution.py:41
  322.7 13.9 %collective-permute-start.19 = (f32[32,1024]{1,0:T(8,128)S(1)}, f32[32,1024]{1,0:T(8,128)S(1)}, u32[]{:S(2)}, u32[]{:S(2)}) collective-permute-start(f32[32,1024]{1,0:T(8,128)S(1)} %get-tuple-element.218), channel_id=1, source_target_pairs={{0,16},{2,18},{4,20},{6,22},{8,24},{10,26},{12,28},{14,30},{16,0},... | collective-permute-start | bytes 393224 | tf_op jit(solution)/shard_map/ppermute | solution.py:41
  324.7 14.5 %collective-permute-start.18 = (f32[32,1024]{1,0:T(8,128)S(1)}, f32[32,1024]{1,0:T(8,128)S(1)}, u32[]{:S(2)}, u32[]{:S(2)}) collective-permute-start(f32[32,1024]{1,0:T(8,128)S(1)} %get-tuple-element.216), channel_id=1, source_target_pairs={{0,8},{2,10},{4,12},{6,14},{8,0},{10,2},{12,4},{14,6},{16,24},{18,... | collective-permute-start | bytes 393224 | tf_op jit(solution)/shard_map/ppermute | solution.py:41
  326.7 12.6 %collective-permute-start.10 = (f32[32,1024]{1,0:T(8,128)S(1)}, f32[32,1024]{1,0:T(8,128)S(1)}, u32[]{:S(2)}, u32[]{:S(2)}) collective-permute-start(f32[32,1024]{1,0:T(8,128)S(1)} %get-tuple-element.214), channel_id=1, source_target_pairs={{0,24},{2,26},{4,28},{6,30},{8,16},{10,18},{12,20},{14,22},{16,8},... | collective-permute-start | bytes 393224 | tf_op jit(solution)/shard_map/ppermute | solution.py:41
  330.4 19.5 %collective-permute-start.9 = (f32[32,1024]{1,0:T(8,128)S(1)}, f32[32,1024]{1,0:T(8,128)S(1)}, u32[]{:S(2)}, u32[]{:S(2)}) collective-permute-start(f32[32,1024]{1,0:T(8,128)S(1)} %get-tuple-element.215), channel_id=1, source_target_pairs={{0,16},{2,18},{4,20},{6,22},{8,24},{10,26},{12,28},{14,30},{16,0},... | collective-permute-start | bytes 393224 | tf_op jit(solution)/shard_map/ppermute | solution.py:41
  334.8 19.8 %collective-permute-start.8 = (f32[32,1024]{1,0:T(8,128)S(1)}, f32[32,1024]{1,0:T(8,128)S(1)}, u32[]{:S(2)}, u32[]{:S(2)}) collective-permute-start(f32[32,1024]{1,0:T(8,128)S(1)} %get-tuple-element.213), channel_id=1, source_target_pairs={{0,8},{2,10},{4,12},{6,14},{8,0},{10,2},{12,4},{14,6},{16,24},{18,... | collective-permute-start | bytes 393224 | tf_op jit(solution)/shard_map/ppermute | solution.py:41
  336.6 18.1 %collective-permute-start.70 = (f32[32,1024]{1,0:T(8,128)S(1)}, f32[32,1024]{1,0:T(8,128)S(1)}, u32[]{:S(2)}, u32[]{:S(2)}) collective-permute-start(f32[32,1024]{1,0:T(8,128)S(1)} %get-tuple-element.205), channel_id=1, source_target_pairs={{0,24},{2,26},{4,28},{6,30},{8,16},{10,18},{12,20},{14,22},{16,8},... | collective-permute-start | bytes 393224 | tf_op jit(solution)/shard_map/ppermute | solution.py:41
  339.2 19.8 %collective-permute-start.69 = (f32[32,1024]{1,0:T(8,128)S(1)}, f32[32,1024]{1,0:T(8,128)S(1)}, u32[]{:S(2)}, u32[]{:S(2)}) collective-permute-start(f32[32,1024]{1,0:T(8,128)S(1)} %get-tuple-element.206), channel_id=1, source_target_pairs={{0,16},{2,18},{4,20},{6,22},{8,24},{10,26},{12,28},{14,30},{16,0},... | collective-permute-start | bytes 393224 | tf_op jit(solution)/shard_map/ppermute | solution.py:41
  339.3 19.7 %collective-permute-start.68 = (f32[32,1024]{1,0:T(8,128)S(1)}, f32[32,1024]{1,0:T(8,128)S(1)}, u32[]{:S(2)}, u32[]{:S(2)}) collective-permute-start(f32[32,1024]{1,0:T(8,128)S(1)} %get-tuple-element.204), channel_id=1, source_target_pairs={{0,8},{2,10},{4,12},{6,14},{8,0},{10,2},{12,4},{14,6},{16,24},{18,... | collective-permute-start | bytes 393224 | tf_op jit(solution)/shard_map/ppermute | solution.py:41
  349.9 14.3 %collective-permute-start.60 = (f32[32,1024]{1,0:T(8,128)S(1)}, f32[32,1024]{1,0:T(8,128)S(1)}, u32[]{:S(2)}, u32[]{:S(2)}) collective-permute-start(f32[32,1024]{1,0:T(8,128)S(1)} %get-tuple-element.202), channel_id=1, source_target_pairs={{0,24},{2,26},{4,28},{6,30},{8,16},{10,18},{12,20},{14,22},{16,8},... | collective-permute-start | bytes 393224 | tf_op jit(solution)/shard_map/ppermute | solution.py:41
  354.6 13.6 %collective-permute-start.59 = (f32[32,1024]{1,0:T(8,128)S(1)}, f32[32,1024]{1,0:T(8,128)S(1)}, u32[]{:S(2)}, u32[]{:S(2)}) collective-permute-start(f32[32,1024]{1,0:T(8,128)S(1)} %get-tuple-element.203), channel_id=1, source_target_pairs={{0,16},{2,18},{4,20},{6,22},{8,24},{10,26},{12,28},{14,30},{16,0},... | collective-permute-start | bytes 393224 | tf_op jit(solution)/shard_map/ppermute | solution.py:41
  354.7 13.5 %collective-permute-start.58 = (f32[32,1024]{1,0:T(8,128)S(1)}, f32[32,1024]{1,0:T(8,128)S(1)}, u32[]{:S(2)}, u32[]{:S(2)}) collective-permute-start(f32[32,1024]{1,0:T(8,128)S(1)} %get-tuple-element.201), channel_id=1, source_target_pairs={{0,8},{2,10},{4,12},{6,14},{8,0},{10,2},{12,4},{14,6},{16,24},{18,... | collective-permute-start | bytes 393224 | tf_op jit(solution)/shard_map/ppermute | solution.py:41
  358.9 13.2 %collective-permute-start.21 = (bf16[32,1024]{1,0:T(8,128)(2,1)S(1)}, bf16[32,1024]{1,0:T(8,128)(2,1)S(1)}, u32[]{:S(2)}, u32[]{:S(2)}) collective-permute-start(bf16[32,1024]{1,0:T(8,128)(2,1)S(1)} %get-tuple-element.154), channel_id=1, source_target_pairs={{0,8},{2,10},{4,12},{6,14},{8,0},{10,2},{12,4},{14,6},{16,24},{18,... | collective-permute-start | bytes 196616 | tf_op jit(solution)/shard_map/ppermute | solution.py:41
  359.0 13.8 %collective-permute-start.22 = (bf16[32,1024]{1,0:T(8,128)(2,1)S(1)}, bf16[32,1024]{1,0:T(8,128)(2,1)S(1)}, u32[]{:S(2)}, u32[]{:S(2)}) collective-permute-start(bf16[32,1024]{1,0:T(8,128)(2,1)S(1)} %get-tuple-element.154), channel_id=1, source_target_pairs={{0,16},{2,18},{4,20},{6,22},{8,24},{10,26},{12,28},{14,30},{16,0},... | collective-permute-start | bytes 196616 | tf_op jit(solution)/shard_map/ppermute | solution.py:41
  384.9 11.4 %collective-permute-start.14 = (bf16[128,1024]{1,0:T(8,128)(2,1)S(1)}, bf16[128,1024]{1,0:T(8,128)(2,1)S(1)}, u32[]{:S(2)}, u32[]{:S(2)}) collective-permute-start(bf16[128,1024]{1,0:T(8,128)(2,1)S(1)} %constant_dynamic-update-slice_fusion.82), channel_id=1, source_target_pairs={{0,4},{2,6},{4,0},{6,2},{8,12},{10,14},{12,8},{14,10},{16,20},{18,... | collective-permute-start | bytes 786440 | tf_op jit(solution)/shard_map/ppermute | solution.py:41
  389.9 11.8 %collective-permute-start.64 = (bf16[128,1024]{1,0:T(8,128)(2,1)S(1)}, bf16[128,1024]{1,0:T(8,128)(2,1)S(1)}, u32[]{:S(2)}, u32[]{:S(2)}) collective-permute-start(bf16[128,1024]{1,0:T(8,128)(2,1)S(1)} %constant_dynamic-update-slice_fusion.46), channel_id=1, source_target_pairs={{0,4},{2,6},{4,0},{6,2},{8,12},{10,14},{12,8},{14,10},{16,20},{18,... | collective-permute-start | bytes 786440 | tf_op jit(solution)/shard_map/ppermute | solution.py:41
  393.6 17.5 %collective-permute-start.25 = (bf16[256,1024]{1,0:T(8,128)(2,1)S(1)}, bf16[256,1024]{1,0:T(8,128)(2,1)S(1)}, u32[]{:S(2)}, u32[]{:S(2)}) collective-permute-start(bf16[256,1024]{1,0:T(8,128)(2,1)S(1)} %constant_dynamic-update-slice_fusion.72), channel_id=1, source_target_pairs={{0,4},{2,6},{4,0},{6,2},{8,12},{10,14},{12,8},{14,10},{16,20},{18,... | collective-permute-start | bytes 1572872 | tf_op jit(solution)/shard_map/ppermute | solution.py:41
  396.3 14.8 %collective-permute-start.15 = (bf16[256,1024]{1,0:T(8,128)(2,1)S(1)}, bf16[256,1024]{1,0:T(8,128)(2,1)S(1)}, u32[]{:S(2)}, u32[]{:S(2)}) collective-permute-start(bf16[256,1024]{1,0:T(8,128)(2,1)S(1)} %constant_dynamic-update-slice_fusion.80), channel_id=1, source_target_pairs={{0,2},{2,0},{4,6},{6,4},{8,10},{10,8},{12,14},{14,12},{16,18},{18,... | collective-permute-start | bytes 1572872 | tf_op jit(solution)/shard_map/ppermute | solution.py:41
  399.2 17.5 %collective-permute-start.75 = (bf16[256,1024]{1,0:T(8,128)(2,1)S(1)}, bf16[256,1024]{1,0:T(8,128)(2,1)S(1)}, u32[]{:S(2)}, u32[]{:S(2)}) collective-permute-start(bf16[256,1024]{1,0:T(8,128)(2,1)S(1)} %constant_dynamic-update-slice_fusion.36), channel_id=1, source_target_pairs={{0,4},{2,6},{4,0},{6,2},{8,12},{10,14},{12,8},{14,10},{16,20},{18,... | collective-permute-start | bytes 1572872 | tf_op jit(solution)/shard_map/ppermute | solution.py:41
  401.7 17.4 %collective-permute-start.65 = (bf16[256,1024]{1,0:T(8,128)(2,1)S(1)}, bf16[256,1024]{1,0:T(8,128)(2,1)S(1)}, u32[]{:S(2)}, u32[]{:S(2)}) collective-permute-start(bf16[256,1024]{1,0:T(8,128)(2,1)S(1)} %constant_dynamic-update-slice_fusion.44), channel_id=1, source_target_pairs={{0,2},{2,0},{4,6},{6,4},{8,10},{10,8},{12,14},{14,12},{16,18},{18,... | collective-permute-start | bytes 1572872 | tf_op jit(solution)/shard_map/ppermute | solution.py:41
  459.9 24.4 %collective-permute-start.36 = (bf16[256,1024]{1,0:T(8,128)(2,1)}, bf16[256,1024]{1,0:T(8,128)(2,1)}, u32[]{:S(2)}, u32[]{:S(2)}) collective-permute-start(bf16[256,1024]{1,0:T(8,128)(2,1)} %dynamic-slice_convert_fusion.2), channel_id=1, source_target_pairs={{0,4},{2,6},{4,0},{6,2},{8,12},{10,14},{12,8},{14,10},{16,20},{18,... | collective-permute-start | bytes 1572872 | tf_op jit(solution)/shard_map/ppermute | solution.py:41
  462.6 46.6 %collective-permute-start.26 = (bf16[256,1024]{1,0:T(8,128)(2,1)}, bf16[256,1024]{1,0:T(8,128)(2,1)}, u32[]{:S(2)}, u32[]{:S(2)}) collective-permute-start(bf16[256,1024]{1,0:T(8,128)(2,1)} %dynamic-slice_convert_fusion.3), channel_id=1, source_target_pairs={{0,2},{2,0},{4,6},{6,4},{8,10},{10,8},{12,14},{14,12},{16,18},{18,... | collective-permute-start | bytes 1572872 | tf_op jit(solution)/shard_map/ppermute | solution.py:41
  467.6 15.2 %collective-permute-start.46 = (f32[512,256]{0,1:T(8,128)}, f32[512,256]{0,1:T(8,128)}, u32[]{:S(2)}, u32[]{:S(2)}) collective-permute-start(f32[512,256]{0,1:T(8,128)} %constant_dynamic-slice_fusion.13), channel_id=1, source_target_pairs={{0,2},{2,0},{4,6},{6,4},{8,10},{10,8},{12,14},{14,12},{16,18},{18,... | collective-permute-start | bytes 1572872 | tf_op jit(solution)/shard_map/ppermute | solution.py:41
  496.9 24.7 %collective-permute-start.37 = (f32[128,1024]{1,0:T(8,128)}, f32[128,1024]{1,0:T(8,128)}, u32[]{:S(2)}, u32[]{:S(2)}) collective-permute-start(f32[128,1024]{1,0:T(8,128)} %constant_dynamic-slice_fusion.17), channel_id=1, source_target_pairs={{0,2},{2,0},{4,6},{6,4},{8,10},{10,8},{12,14},{14,12},{16,18},{18,... | collective-permute-start | bytes 1572872 | tf_op jit(solution)/shard_map/ppermute | solution.py:41
  521.2 35.2 %collective-permute-start.55 = (bf16[512,256]{0,1:T(8,128)(2,1)S(1)}, bf16[512,256]{0,1:T(8,128)(2,1)S(1)}, u32[]{:S(2)}, u32[]{:S(2)}) collective-permute-start(bf16[512,256]{0,1:T(8,128)(2,1)S(1)} %constant_dynamic-update-slice_fusion.52), channel_id=1, source_target_pairs={{0,2},{2,0},{4,6},{6,4},{8,10},{10,8},{12,14},{14,12},{16,18},{18,... | collective-permute-start | bytes 786440 | tf_op jit(solution)/shard_map/ppermute | solution.py:41
  523.9 13.8 %collective-permute-start.39 = (f32[32,1024]{1,0:T(8,128)S(1)}, f32[32,1024]{1,0:T(8,128)S(1)}, u32[]{:S(2)}, u32[]{:S(2)}) collective-permute-start(f32[32,1024]{1,0:T(8,128)S(1)} %get-tuple-element.212), channel_id=1, source_target_pairs={{0,16},{2,18},{4,20},{6,22},{8,24},{10,26},{12,28},{14,30},{16,0},... | collective-permute-start | bytes 393224 | tf_op jit(solution)/shard_map/ppermute | solution.py:41
  523.9 13.8 %collective-permute-start.38 = (f32[32,1024]{1,0:T(8,128)S(1)}, f32[32,1024]{1,0:T(8,128)S(1)}, u32[]{:S(2)}, u32[]{:S(2)}) collective-permute-start(f32[32,1024]{1,0:T(8,128)S(1)} %get-tuple-element.210), channel_id=1, source_target_pairs={{0,8},{2,10},{4,12},{6,14},{8,0},{10,2},{12,4},{14,6},{16,24},{18,... | collective-permute-start | bytes 393224 | tf_op jit(solution)/shard_map/ppermute | solution.py:41
  527.4 12.4 %collective-permute-start.30 = (f32[32,1024]{1,0:T(8,128)S(1)}, f32[32,1024]{1,0:T(8,128)S(1)}, u32[]{:S(2)}, u32[]{:S(2)}) collective-permute-start(f32[32,1024]{1,0:T(8,128)S(1)} %get-tuple-element.208), channel_id=1, source_target_pairs={{0,24},{2,26},{4,28},{6,30},{8,16},{10,18},{12,20},{14,22},{16,8},... | collective-permute-start | bytes 393224 | tf_op jit(solution)/shard_map/ppermute | solution.py:41
  530.5 12.8 %collective-permute-start.29 = (f32[32,1024]{1,0:T(8,128)S(1)}, f32[32,1024]{1,0:T(8,128)S(1)}, u32[]{:S(2)}, u32[]{:S(2)}) collective-permute-start(f32[32,1024]{1,0:T(8,128)S(1)} %get-tuple-element.209), channel_id=1, source_target_pairs={{0,16},{2,18},{4,20},{6,22},{8,24},{10,26},{12,28},{14,30},{16,0},... | collective-permute-start | bytes 393224 | tf_op jit(solution)/shard_map/ppermute | solution.py:41
  558.2 13.9 %collective-permute-start.45 = (bf16[256,1024]{1,0:T(8,128)(2,1)S(1)}, bf16[256,1024]{1,0:T(8,128)(2,1)}, u32[]{:S(2)}, u32[]{:S(2)}) collective-permute-start(bf16[256,1024]{1,0:T(8,128)(2,1)S(1)} %constant_dynamic-update-slice_fusion.56), channel_id=1, source_target_pairs={{0,4},{2,6},{4,0},{6,2},{8,12},{10,14},{12,8},{14,10},{16,20},{18,... | collective-permute-start | bytes 1572872 | tf_op jit(solution)/shard_map/ppermute | solution.py:41
  561.4 13.8 %collective-permute-start.35 = (bf16[256,1024]{1,0:T(8,128)(2,1)}, bf16[256,1024]{1,0:T(8,128)(2,1)S(1)}, u32[]{:S(2)}, u32[]{:S(2)}) collective-permute-start(bf16[256,1024]{1,0:T(8,128)(2,1)} %constant_dynamic-update-slice_fusion.64), channel_id=1, source_target_pairs={{0,2},{2,0},{4,6},{6,4},{8,10},{10,8},{12,14},{14,12},{16,18},{18,... | collective-permute-start | bytes 1572872 | tf_op jit(solution)/shard_map/ppermute | solution.py:41
  (185 other events, 1720.8 us)
Sparse Core Ops, SparseCore 0:
  9.6 11.7 all-gather.4
  143.0 10.2 all-gather.6
  284.9 8.2 reduce-scatter.5
  297.8 10.7 reduce-scatter.3
  472.4 9.2 reduce-scatter.7
